TPU v7x, 128 devices: a whole 4x4x4 slice. The times are simulated.
128 devices in a mesh: row: 16 (over x_lo, z, core), col: 8 (over x_hi, y).
Axes of the slice: x: 4 (x_hi: 2, x_lo: 2; x = x_hi * 2 + x_lo), y: 4, z: 4, core: 2. Of those that a mesh axis runs over, the one named last changes fastest.
Arguments:
- matrix_tiles: float32 [5, 16, 128, 10, 8, 128], P(None, 'row', None, None, 'col'), may hold values from -60715.73 to 60715.73
Outputs:
- reduced: float32 [5, 16, 128, 10, 8, 128], P(None, 'row', None, None, 'col')
All inputs are finite; a program needn't handle non-finite values.
Results may differ from a plain program's by a relative error of at most 0.0003.
Values sent between devices are 32-bit elements; how exact they have to be, the bound alone decides.
No kernel may reach another device: no remote copies, remote signals or barrier semaphores. Data moves between devices by JAX's collectives and lax.ppermute only.
A program may use at most 128 MiB of HBM per device.

v0:
```python
import jax
import jax.numpy as jnp
from jax import lax
from jax.sharding import Mesh
from jax.sharding import PartitionSpec as P

BAND = 256
PANELS = 2
ROW = ("row_0", "row_1", "row_2")


def broadcast(shard, axis, root):
    return lax.dynamic_index_in_dim(lax.all_gather(shard, axis), root, 0, keepdims=False)


def filled_up(lines, peers):
    spare = -len(lines) % peers
    return jnp.pad(lines, [(0, spare)] + [(0, 0)] * (lines.ndim - 1))


def sent_to_all(shard, axis):
    peers = lax.axis_size(axis)
    return lax.all_to_all(
        jnp.broadcast_to(shard[None], (peers, *shard.shape)), axis, 0, 0, tiled=True
    )


def joined_along(blocks, dim):
    lengths = list(blocks.shape[1:])
    lengths[dim] *= blocks.shape[0]
    return jnp.moveaxis(blocks, 0, dim).reshape(lengths)


def collect(shard, axis, dim):
    blocks = sent_to_all(shard, axis)
    return joined_along(blocks, dim)


def cut_along(shard, dim, peers):
    before, after = (shard.shape[:dim], shard.shape[dim + 1 :])
    return jnp.moveaxis(shard.reshape(*before, peers, -1, *after), dim, 0)


def sum_at_owner(shard, axis, dim):
    blocks = cut_along(shard, dim, lax.axis_size(axis))
    arrived = lax.all_to_all(blocks, axis, split_axis=0, concat_axis=0, tiled=True)
    return arrived.sum(axis=0)


def nested_sum(shard, axes):
    padded = filled_up(shard, lax.axis_size(axes))
    whole = collect(sum_at_owner(padded, axes, 0), axes, 0)
    return lax.slice_in_dim(whole, 0, len(shard)).reshape(shard.shape)


def in_one(arrays, axis):
    ends = [0]
    for a in arrays:
        ends.append(ends[-1] + a.size)
    total = nested_sum(jnp.concatenate([a.ravel() for a in arrays]), axis)
    return tuple((total[b:e].reshape(a.shape) for a, b, e in zip(arrays, ends, ends[1:])))


def over_copies(shard, axis):
    everything = sent_to_all(shard, axis)
    return jnp.sum(everything, axis=0)


def sum_by_parts(shard, axes):
    lines = shard.reshape(-1, shard.shape[-1])
    own = sum_at_owner(filled_up(lines, lax.axis_size(axes)), axes, 0)
    whole = collect(own, axes, 0)
    return whole[: len(lines)].reshape(shard.shape)


def summed_rows_2(shard, axes, dim):
    far, near = axes
    blocks = cut_along(shard, dim, lax.axis_size(far))
    nearer = sum_at_owner(blocks, near, dim + 1)
    arrived = lax.all_to_all(nearer, far, split_axis=0, concat_axis=0, tiled=True)
    return arrived.sum(axis=0)


def gather_axes(shard, axes, dim):
    far, near = axes
    blocks = sent_to_all(sent_to_all(shard, far), near)
    return joined_along(blocks.swapaxes(0, 1).reshape(-1, *shard.shape), dim)


def sum_by_parts_2(shard, axes):
    lines = shard.reshape(-1, shard.shape[-1])
    own = summed_rows_2(filled_up(lines, lax.axis_size(axes[0]) * lax.axis_size(axes[1])), axes, 0)
    whole = gather_axes(own, axes, 0)
    return whole[: len(lines)].reshape(shard.shape)


def multiply(first_matrix, second_matrix):
    return jnp.dot(
        first_matrix,
        second_matrix,
        precision=lax.Precision.HIGHEST,
        preferred_element_type=first_matrix.dtype,
    )


def transposed_left(first_matrix, second_matrix):
    return lax.dot_general(
        first_matrix,
        second_matrix,
        (((0,), (0,)), ((), ())),
        precision=lax.Precision.HIGHEST,
        preferred_element_type=first_matrix.dtype,
    )


def transposed_right(first_matrix, second_matrix):
    return lax.dot_general(
        first_matrix,
        second_matrix,
        (((1,), (1,)), ((), ())),
        precision=lax.Precision.HIGHEST,
        preferred_element_type=first_matrix.dtype,
    )


def lower_inverse(matrix):
    factor = jnp.linalg.cholesky(matrix)
    identity = jnp.eye(matrix.shape[0], dtype=matrix.dtype)
    return lax.linalg.triangular_solve(factor, identity, left_side=True, lower=True)


def reflector_factors(gram_matrix, top_panel):
    inverse = lower_inverse(gram_matrix)
    top_basis = transposed_right(top_panel, inverse)
    sign_values = jnp.where(jnp.diagonal(top_basis) >= 0, -1.0, 1.0).astype(top_basis.dtype)
    shifted = top_basis - jnp.diag(sign_values)
    outer_inverse = lower_inverse(transposed_left(shifted, shifted))
    kernel = transposed_left(outer_inverse, outer_inverse)
    transform = -sign_values[:, None] * multiply(shifted, kernel)
    return (inverse, sign_values, transform)


def mirror_order(pieces, block_rows, tile_size):
    stacked = jnp.stack(pieces, 0)
    stacked = stacked.reshape(len(pieces), block_rows, tile_size, stacked.shape[-1])
    return stacked.transpose(1, 0, 2, 3).reshape(-1, stacked.shape[-1])


def on_device(matrix_tiles):
    tile_shape = matrix_tiles.shape
    block_rows = tile_shape[0]
    tile_size = tile_shape[2]
    block_cols = tile_shape[3]
    row_count = block_rows * tile_size
    col_count = block_cols * tile_size
    local_block = matrix_tiles.reshape(row_count, col_count)
    row_devices = lax.axis_size(ROW)
    col_devices = lax.axis_size("col")
    row_ratio = row_devices // col_devices
    row_index = lax.axis_index(ROW)
    col_index = lax.axis_index("col")
    positions = jnp.arange(row_count, dtype=jnp.int32)
    global_rows = (
        positions // tile_size * row_devices + row_index
    ) * tile_size + positions % tile_size
    band_columns = jnp.arange(BAND, dtype=jnp.int32)
    panel_tiles = BAND // tile_size
    for panel_index in range(PANELS):
        panel_start = panel_index * BAND
        below_start = panel_start + BAND
        pieces = []
        for offset in range(panel_tiles):
            column_tile = panel_start // tile_size + offset
            local_tile = column_tile // col_devices
            source = local_block[:, local_tile * tile_size : (local_tile + 1) * tile_size]
            pieces.append(broadcast(source, "col", column_tile % col_devices))
        panel_rows = jnp.concatenate(pieces, 1)
        panel_rows = jnp.where((global_rows >= below_start)[:, None], panel_rows, 0.0)
        partial_gram = transposed_left(panel_rows, panel_rows)
        blocks = []
        for offset in range(panel_tiles):
            row_tile = below_start // tile_size + offset
            local_tile = row_tile // row_devices
            owner_flag = (row_index == row_tile % row_devices).astype(local_block.dtype)
            blocks.append(
                panel_rows[local_tile * tile_size : (local_tile + 1) * tile_size] * owner_flag
            )
        gram_matrix, top_panel = in_one((partial_gram, jnp.concatenate(blocks, 0)), ROW)
        inverse, sign_values, transform = reflector_factors(gram_matrix, top_panel)
        sign_places = (global_rows[:, None] - below_start == band_columns[None, :]).astype(
            local_block.dtype
        )
        vec_rows = transposed_right(panel_rows, inverse) - sign_places * sign_values[None, :]
        pieces = []
        for part_index in range(row_ratio):
            pieces.append(broadcast(vec_rows, ROW, col_index + col_devices * part_index))
        vec_cols = mirror_order(pieces, block_rows, tile_size)
        summed_rows = over_copies(multiply(local_block, vec_cols), "col")
        applied = multiply(summed_rows, transform)
        inner_term = multiply(transform.T, sum_by_parts(transposed_left(vec_rows, applied), ROW))
        update_rows = applied - 0.5 * multiply(vec_rows, inner_term)
        column_part = transposed_left(local_block, vec_rows)
        summed_cols = sum_by_parts_2(column_part, (("row_0", "row_1"), "row_2"))
        update_cols = multiply(summed_cols, transform) - 0.5 * multiply(vec_cols, inner_term)
        left_factor = jnp.concatenate([vec_rows, update_rows], 1)
        right_factor = jnp.concatenate([update_cols, vec_cols], 1)
        local_block = local_block - transposed_right(left_factor, right_factor)
    return local_block.reshape(tile_shape)


def solution(mesh):
    finer = Mesh(
        mesh.devices.reshape(2, 4, 2, mesh.shape["col"]), ("row_0", "row_1", "row_2", "col")
    )
    return jax.shard_map(
        on_device,
        mesh=finer,
        in_specs=(P(None, ROW, None, None, "col", None),),
        out_specs=P(None, ROW, None, None, "col", None),
        check_vma=False,
    )
```

profile of v0, /device:TPU:1, one launch (start us, length us, event | category | flops | bytes accessed | tf_op | source)
XLA Modules:
  0.0 931.5 jit_solution(12975293297343622348)
XLA Ops:
  6.5 12.1 %reduce.10 = f32[5,128,10,128]{3,2,1,0:T(8,128)} reduce(f32[5,1,128,10,1,128]{5,4,3,2,1,0:T(1,128)} %param.4, f32[]{:T(128)} %constant.242), dimensions={1,4}, to_apply=%param.4.reduce_sub_computation | reduce | bytes 6553604 | tf_op args[0]
  22.7 14.1 %copy.72 = f32[640,1280]{0,1:T(8,128)} copy(f32[640,1280]{1,0:T(8,128)S(1)} %bitcast.211) | data formatting | bytes 6553600 | tf_op jit(solution)/shard_map/reshape | solution.py:156
  38.6 60.9 %all-gather.9.cloned.1.call-done = f32[5120,128]{0,1:T(8,128)} async-done(((f32[640,128]{0,1:T(8,128)}), f32[5120,128]{0,1:T(8,128)}) %all-gather.9.cloned.1.call-update) | async-done | bytes 2621456 | tf_op jit(solution)/shard_map/all_gather | solution.py:13
  113.8 9.9 %all-to-all-done = f32[16,1,8192]{2,1,0:T(1,128)} async-done(((f32[16,1,8192]{2,1,0:T(1,128)}), f32[16,1,8192]{2,1,0:T(1,128)}, u32[]{:S(2)}, u32[]{:S(2)}) %all-to-all-start) | async-done | bytes 524320 | tf_op jit(solution)/shard_map/all_to_all | solution.py:46
  131.6 9.9 %all-to-all-done.1 = f32[16,1,8192]{2,1,0:T(1,128)} async-done(((f32[16,1,8192]{2,1,0:T(1,128)}), f32[16,1,8192]{2,1,0:T(1,128)}, u32[]{:S(2)}, u32[]{:S(2)}) %all-to-all-start.1) | async-done | bytes 524320 | tf_op jit(solution)/shard_map/all_to_all | solution.py:23
  150.6 13.2 %cholesky.214 = f32[128,128]{1,0:T(8,128)} custom-call(f32[128,128]{1,0:T(8,128)} %cholesky.346), custom_call_target="Cholesky" | custom-call | tf_op jit(solution)/shard_map/jit(cholesky)/cholesky | solution.py:127
  165.2 11.3 %custom-call.21 = f32[1,128,128]{1,2,0:T(8,128)} custom-call(f32[1,128,128]{2,1,0:T(8,128)} %get-tuple-element.108), custom_call_target="InvertDiagBlocksLowerTriangular" | custom-call | tf_op jit(solution)/shard_map/jit(cholesky)/cholesky | solution.py:127
  181.5 13.2 %cholesky.231 = f32[128,128]{1,0:T(8,128)} custom-call(f32[128,128]{1,0:T(8,128)} %convolution_subtract_fusion.11), custom_call_target="Cholesky" | custom-call | tf_op jit(solution)/shard_map/jit(cholesky)/cholesky | solution.py:127
  207.7 21.1 %custom-call.22 = f32[2,128,128]{1,2,0:T(8,128)} custom-call(f32[2,128,128]{2,1,0:T(8,128)} %get-tuple-element.33), custom_call_target="InvertDiagBlocksLowerTriangular" | custom-call | tf_op jit(solution)/shard_map/triangular_solve/custom-call.0 | solution.py:129
  265.5 16.7 %all-to-all-done.6 = f32[8,80,256]{2,1,0:T(8,128)} async-done(((f32[8,80,256]{2,1,0:T(8,128)}), f32[8,80,256]{2,1,0:T(8,128)}, u32[]{:S(2)}, u32[]{:S(2)}) %all-to-all-start.6) | async-done | bytes 655392 | tf_op jit(solution)/shard_map/all_to_all | solution.py:80
  290.3 25.9 %all-gather.11.cloned.1.call-done = f32[10240,256]{0,1:T(8,128)} async-done(((f32[640,256]{0,1:T(8,128)}), f32[10240,256]{0,1:T(8,128)}) %all-gather.11.cloned.1.call-update) | async-done | bytes 10485776 | tf_op jit(solution)/shard_map/all_gather | solution.py:13
  316.3 11.4 %copy.91 = f32[10240,256]{1,0:T(8,128)} copy(f32[10240,256]{0,1:T(8,128)} %all-gather.11.cloned.1.call-done) | data formatting | bytes 20971520 | tf_op jit(solution)/shard_map/all_gather | solution.py:13
  349.4 11.7 %cholesky.248 = f32[128,128]{1,0:T(8,128)S(1)} custom-call(f32[128,128]{1,0:T(8,128)S(1)} %cholesky.349), custom_call_target="Cholesky" | custom-call | tf_op jit(solution)/shard_map/jit(cholesky)/cholesky | solution.py:127
  361.2 9.8 %custom-call.23 = f32[1,128,128]{1,2,0:T(8,128)S(1)} custom-call(f32[1,128,128]{2,1,0:T(8,128)S(1)} %get-tuple-element.104), custom_call_target="InvertDiagBlocksLowerTriangular" | custom-call | tf_op jit(solution)/shard_map/jit(cholesky)/cholesky | solution.py:127
  371.5 11.7 %cholesky.265 = f32[128,128]{1,0:T(8,128)S(1)} custom-call(f32[128,128]{1,0:T(8,128)S(1)} %convolution_subtract_fusion.10), custom_call_target="Cholesky" | custom-call | tf_op jit(solution)/shard_map/jit(cholesky)/cholesky | solution.py:127
  389.7 19.9 %custom-call.24 = f32[2,128,128]{1,2,0:T(8,128)S(1)} custom-call(f32[2,128,128]{2,1,0:T(8,128)S(1)} %get-tuple-element.34), custom_call_target="InvertDiagBlocksLowerTriangular" | custom-call | tf_op jit(solution)/shard_map/triangular_solve/custom-call.0 | solution.py:129
  459.7 58.3 %all-gather.13.cloned.1.call-done = f32[5120,128]{0,1:T(8,128)} async-done(((f32[640,128]{0,1:T(8,128)}), f32[5120,128]{0,1:T(8,128)}) %all-gather.13.cloned.1.call-update) | async-done | bytes 2621456 | tf_op jit(solution)/shard_map/all_gather | solution.py:13
  526.0 15.2 %all_to_all.102 = f32[16,1,8192]{2,1,0:T(1,128)} all-to-all(f32[16,1,8192]{2,1,0:T(1,128)S(1)} %copy.75), channel_id=1, replica_groups=mesh['row_0'=2,'row_1'=4,'row_2'=2,'col'=8] {'row_0','row_1','row_2'}, dimensions={0} | all-to-all | bytes 1048576 | tf_op jit(solution)/shard_map/all_to_all | solution.py:46
  549.0 9.9 %all-to-all-done.10 = f32[16,1,8192]{2,1,0:T(1,128)} async-done(((f32[16,1,8192]{2,1,0:T(1,128)}), f32[16,1,8192]{2,1,0:T(1,128)}, u32[]{:S(2)}, u32[]{:S(2)}) %all-to-all-start.10) | async-done | bytes 524320 | tf_op jit(solution)/shard_map/all_to_all | solution.py:23
  565.7 12.3 %cholesky.282 = f32[128,128]{1,0:T(8,128)} custom-call(f32[128,128]{1,0:T(8,128)S(1)} %cholesky.352), custom_call_target="Cholesky" | custom-call | tf_op jit(solution)/shard_map/jit(cholesky)/cholesky | solution.py:127
  581.1 11.3 %custom-call.25 = f32[1,128,128]{1,2,0:T(8,128)} custom-call(f32[1,128,128]{2,1,0:T(8,128)} %get-tuple-element.100), custom_call_target="InvertDiagBlocksLowerTriangular" | custom-call | tf_op jit(solution)/shard_map/jit(cholesky)/cholesky | solution.py:127
  595.8 13.2 %cholesky.299 = f32[128,128]{1,0:T(8,128)} custom-call(f32[128,128]{1,0:T(8,128)} %convolution_subtract_fusion.9), custom_call_target="Cholesky" | custom-call | tf_op jit(solution)/shard_map/jit(cholesky)/cholesky | solution.py:127
  615.4 8.6 while.10
  624.0 21.1 %custom-call.26 = f32[2,128,128]{1,2,0:T(8,128)} custom-call(f32[2,128,128]{2,1,0:T(8,128)} %get-tuple-element.35), custom_call_target="InvertDiagBlocksLowerTriangular" | custom-call | tf_op jit(solution)/shard_map/triangular_solve/custom-call.0 | solution.py:129
  672.1 21.9 %all_to_all.103 = f32[8,80,256]{2,1,0:T(8,128)} all-to-all(f32[8,80,256]{2,1,0:T(8,128)} %reduce_sum.98), channel_id=1, replica_groups=mesh['row_0'=2,'row_1'=4,'row_2'=2,'col'=8] {'row_0','row_1'}, dimensions={0} | all-to-all | bytes 1310720 | tf_op jit(solution)/shard_map/all_to_all | solution.py:80
  701.9 30.8 %all-gather.15.cloned.1.call-done = f32[10240,256]{0,1:T(8,128)} async-done(((f32[640,256]{0,1:T(8,128)}), f32[10240,256]{0,1:T(8,128)}) %all-gather.15.cloned.1.call-update) | async-done | bytes 10485776 | tf_op jit(solution)/shard_map/all_gather | solution.py:13
  732.6 11.4 %copy.92 = f32[10240,256]{1,0:T(8,128)} copy(f32[10240,256]{0,1:T(8,128)} %all-gather.15.cloned.1.call-done) | data formatting | bytes 20971520 | tf_op jit(solution)/shard_map/all_gather | solution.py:13
  769.0 13.2 %cholesky.316 = f32[128,128]{1,0:T(8,128)} custom-call(f32[128,128]{1,0:T(8,128)} %cholesky.355), custom_call_target="Cholesky" | custom-call | tf_op jit(solution)/shard_map/jit(cholesky)/cholesky | solution.py:127
  785.2 11.3 %custom-call.27 = f32[1,128,128]{1,2,0:T(8,128)} custom-call(f32[1,128,128]{2,1,0:T(8,128)} %get-tuple-element.96), custom_call_target="InvertDiagBlocksLowerTriangular" | custom-call | tf_op jit(solution)/shard_map/jit(cholesky)/cholesky | solution.py:127
  799.9 13.2 %cholesky.333 = f32[128,128]{1,0:T(8,128)} custom-call(f32[128,128]{1,0:T(8,128)} %convolution_subtract_fusion.8), custom_call_target="Cholesky" | custom-call | tf_op jit(solution)/shard_map/jit(cholesky)/cholesky | solution.py:127
  827.8 21.3 %custom-call.28 = f32[2,128,128]{1,2,0:T(8,128)} custom-call(f32[2,128,128]{2,1,0:T(8,128)} %get-tuple-element.36), custom_call_target="InvertDiagBlocksLowerTriangular" | custom-call | tf_op jit(solution)/shard_map/triangular_solve/custom-call.0 | solution.py:129
  902.5 9.1 convolution_subtract_fusion
  (278 shorter events, 384.6 us)
Async XLA Ops:
  6.5 93.0 %all-gather.9.cloned.1.call-start = ((), (), s32[]{:S(2)}) async-start(), calls=%async_computation.18 | async-start | bytes 2949120 | tf_op jit(solution)/shard_map/all_gather | solution.py:13
  108.3 15.4 %all-to-all-start = ((f32[16,1,8192]{2,1,0:T(1,128)}), f32[16,1,8192]{2,1,0:T(1,128)}, u32[]{:S(2)}, u32[]{:S(2)}) async-start(f32[16,1,8192]{2,1,0:T(1,128)} %copy.61), calls=%async_computation | async-start | bytes 1048576 | tf_op jit(solution)/shard_map/all_to_all | solution.py:46
  126.3 15.1 %all-to-all-start.1 = ((f32[16,1,8192]{2,1,0:T(1,128)}), f32[16,1,8192]{2,1,0:T(1,128)}, u32[]{:S(2)}, u32[]{:S(2)}) async-start(f32[16,1,8192]{2,1,0:T(1,128)} %broadcast_in_dim.132), calls=%async_computation.1 | async-start | bytes 1048576 | tf_op jit(solution)/shard_map/all_to_all | solution.py:23
  131.5 184.8 %all-gather.11.cloned.1.call-start = ((), (), s32[]{:S(2)}) async-start(), calls=%async_computation.19 | async-start | bytes 11141120 | tf_op jit(solution)/shard_map/all_gather | solution.py:13
  131.6 98.3 %copy-start.11 = (f32[256,256]{1,0:T(8,128)}, f32[256,256]{1,0:T(8,128)S(1)}, u32[]{:S(2)}) copy-start(f32[256,256]{1,0:T(8,128)S(1)} %fusion.28) | copy-start | bytes 786436
  207.7 28.4 %copy-start.25 = (s32[2,2]{1,0:T(2,128)}, s32[2,2]{1,0:T(2,128)S(1)}, u32[]{:S(2)}) copy-start(s32[2,2]{1,0:T(2,128)S(1)} %get-tuple-element.344) | copy-start | bytes 52
  261.3 20.9 %all-to-all-start.6 = ((f32[8,80,256]{2,1,0:T(8,128)}), f32[8,80,256]{2,1,0:T(8,128)}, u32[]{:S(2)}, u32[]{:S(2)}) async-start(f32[8,80,256]{2,1,0:T(8,128)} %reduce_sum.93), calls=%async_computation.6 | async-start | bytes 1310720 | tf_op jit(solution)/shard_map/all_to_all | solution.py:80
  285.7 53.4 %all-to-all-start.7 = ((f32[8,80,256]{2,1,0:T(8,128)}), f32[8,80,256]{2,1,0:T(8,128)}, u32[]{:S(2)}, u32[]{:S(2)}) async-start(f32[8,80,256]{2,1,0:T(8,128)} %broadcast_in_dim.139), calls=%async_computation.7 | async-start | bytes 1310720 | tf_op jit(solution)/shard_map/all_to_all | solution.py:23
  341.9 69.7 %all-to-all-start.2 = ((f32[8,640,256]{2,1,0:T(8,128)}), f32[8,640,256]{2,1,0:T(8,128)}, u32[]{:S(2)}, u32[]{:S(2)}) async-start(f32[8,640,256]{2,1,0:T(8,128)} %broadcast_in_dim.135), calls=%async_computation.2 | async-start | bytes 10485760 | tf_op jit(solution)/shard_map/all_to_all | solution.py:23
  349.4 36.5 %copy-start.26 = (s32[2,2]{1,0:T(2,128)S(1)}, s32[2,2]{1,0:T(2,128)}, u32[]{:S(2)}) copy-start(s32[2,2]{1,0:T(2,128)} %copy-done.25) | copy-start | bytes 52
  361.1 48.4 %copy-start.12 = (f32[256,256]{1,0:T(8,128)S(1)}, f32[256,256]{1,0:T(8,128)}, u32[]{:S(2)}) copy-start(f32[256,256]{1,0:T(8,128)} %copy-done.11) | copy-start | bytes 786436
  413.9 9.7 %all-to-all-start.8 = ((f32[2,8,80,256]{3,2,1,0:T(8,128)}), f32[2,8,80,256]{3,2,1,0:T(8,128)S(1)}, u32[]{:S(2)}, u32[]{:S(2)}) async-start(f32[2,8,80,256]{3,2,1,0:T(8,128)} %broadcast_in_dim.140), calls=%async_computation.8 | async-start | bytes 2621440 | tf_op jit(solution)/shard_map/all_to_all | solution.py:23
  423.6 11.4 %all-to-all-start.3 = ((f32[16,16,256]{2,1,0:T(8,128)}), f32[16,16,256]{2,1,0:T(8,128)S(1)}, u32[]{:S(2)}, u32[]{:S(2)}) async-start(f32[16,16,256]{2,1,0:T(8,128)} %bitcast.16), calls=%async_computation.3 | async-start | bytes 524288 | tf_op jit(solution)/shard_map/all_to_all | solution.py:46
  435.8 11.5 %all-to-all-start.4 = ((f32[16,16,256]{2,1,0:T(8,128)}), f32[16,16,256]{2,1,0:T(8,128)S(1)}, u32[]{:S(2)}, u32[]{:S(2)}) async-start(f32[16,16,256]{2,1,0:T(8,128)} %broadcast_in_dim.138), calls=%async_computation.4 | async-start | bytes 524288 | tf_op jit(solution)/shard_map/all_to_all | solution.py:23
  440.0 77.9 %all-gather.13.cloned.1.call-start = ((), (), s32[]{:S(2)}) async-start(), calls=%async_computation.20 | async-start | bytes 2949120 | tf_op jit(solution)/shard_map/all_gather | solution.py:13
  440.5 3.8 copy-start.6
  447.9 2.3 copy-start.15
  448.8 2.0 copy-start
  448.8 2.2 copy-start.2
  519.1 1.7 copy-start.10
  543.8 15.1 %all-to-all-start.10 = ((f32[16,1,8192]{2,1,0:T(1,128)}), f32[16,1,8192]{2,1,0:T(1,128)}, u32[]{:S(2)}, u32[]{:S(2)}) async-start(f32[16,1,8192]{2,1,0:T(1,128)} %broadcast_in_dim.142), calls=%async_computation.10 | async-start | bytes 1048576 | tf_op jit(solution)/shard_map/all_to_all | solution.py:23
  549.0 183.7 %all-gather.15.cloned.1.call-start = ((), (), s32[]{:S(2)}) async-start(), calls=%async_computation.21 | async-start | bytes 11141120 | tf_op jit(solution)/shard_map/all_gather | solution.py:13
  578.0 67.1 %copy-start.13 = (f32[256,256]{1,0:T(8,128)S(1)}, f32[256,256]{1,0:T(8,128)}, u32[]{:S(2)}) copy-start(f32[256,256]{1,0:T(8,128)} %copy-done.11) | copy-start | bytes 786436
  697.7 55.2 %all-to-all-start.16 = ((f32[8,80,256]{2,1,0:T(8,128)}), f32[8,80,256]{2,1,0:T(8,128)}, u32[]{:S(2)}, u32[]{:S(2)}) async-start(f32[8,80,256]{2,1,0:T(8,128)} %broadcast_in_dim.146), calls=%async_computation.16 | async-start | bytes 1310720 | tf_op jit(solution)/shard_map/all_to_all | solution.py:23
  756.8 97.7 %all-to-all-start.11 = ((f32[8,640,256]{2,1,0:T(8,128)}), f32[8,640,256]{2,1,0:T(8,128)}, u32[]{:S(2)}, u32[]{:S(2)}) async-start(f32[8,640,256]{2,1,0:T(8,128)} %broadcast_in_dim.143), calls=%async_computation.11 | async-start | bytes 10485760 | tf_op jit(solution)/shard_map/all_to_all | solution.py:23
  856.7 13.3 %all-to-all-start.17 = ((f32[2,8,80,256]{3,2,1,0:T(8,128)}), f32[2,8,80,256]{3,2,1,0:T(8,128)}, u32[]{:S(2)}, u32[]{:S(2)}) async-start(f32[2,8,80,256]{3,2,1,0:T(8,128)} %broadcast_in_dim.147), calls=%async_computation.17 | async-start | bytes 2621440 | tf_op jit(solution)/shard_map/all_to_all | solution.py:23
  861.8 3.8 copy-start.19
  865.6 2.9 copy-start.3
  870.0 11.5 %all-to-all-start.12 = ((f32[16,16,256]{2,1,0:T(8,128)}), f32[16,16,256]{2,1,0:T(8,128)}, u32[]{:S(2)}, u32[]{:S(2)}) async-start(f32[16,16,256]{2,1,0:T(8,128)} %bitcast.231), calls=%async_computation.12 | async-start | bytes 524288 | tf_op jit(solution)/shard_map/all_to_all | solution.py:46
  884.6 12.5 %all-to-all-start.13 = ((f32[16,16,256]{2,1,0:T(8,128)}), f32[16,16,256]{2,1,0:T(8,128)}, u32[]{:S(2)}, u32[]{:S(2)}) async-start(f32[16,16,256]{2,1,0:T(8,128)} %broadcast_in_dim.145), calls=%async_computation.13 | async-start | bytes 524288 | tf_op jit(solution)/shard_map/all_to_all | solution.py:23
  897.1 3.9 copy-start.8
  897.1 3.9 copy-start.18
  (13 other events, 14.5 us)
Sparse Core Ops, SparseCore 0:
  38.7 60.7 all-gather.8
  242.6 73.5 all-gather.10
  459.7 58.1 all-gather.12
  659.0 73.5 all-gather.14
where the time goes:
time: 945 us; the launch traced here: 931 us
  other arithmetic  286 us (30%)
  waiting for transfers between devices  235 us (25%)
  local copies, waits for them, and re-layouts  168 us (18%)
  matrix products  102 us (11%)
  starting transfers between devices  69.9 us (7%)
  blocking collectives  50.2 us (5%)
  between operations  19.4 us (2%)
    all_gather x4, waiting for transfers between devices, broadcast(): lax.all_gather(shard, axis)  176 us
    another operation x27, other arithmetic, lower_inverse(): factor = jnp.linalg.cholesky(matrix)  159 us
    another operation x9, other arithmetic, lower_inverse(): lax.linalg.triangular_solve(factor, identity, left_side=True, lower=True)  88.5 us
    all_to_all x10, starting transfers between devices, sent_to_all(): lax.all_to_all(jnp.broadcast_to(shard[None], (peers, *shard.shape)), axis...  51.2 us
    dot_general x14, matrix products, multiply(): jnp.dot(first_matrix, second_matrix, precision=lax.Precision.HIGHEST, pre...  33.8 us
    another operation x29, local copies, waits for them, and re-layouts, lower_inverse(): lax.linalg.triangular_solve(factor, identity, left_side=True, lower=True)  29.4 us
    all_to_all x3, blocking collectives, sum_at_owner(): lax.all_to_all(blocks, axis, split_axis=0, concat_axis=0, tiled=True)  28.3 us
    dot_general x6, matrix products, transposed_right(): lax.dot_general(first_matrix, second_matrix, (((1,), (1,)), ((), ())), pr...  25.5 us
  transfers between devices with their start and end apart: 18, of which 12 were waited for; matrix products, arithmetic and copies ran while one was open for 26% of the time, Pallas kernels for 0%

commit v1 on v0

v1 whole, which is shorter than its diff:
```python
import jax
import jax.numpy as jnp
from jax import lax
from jax.experimental import pallas as pl
from jax.experimental.pallas import tpu as pltpu
from jax.sharding import Mesh
from jax.sharding import PartitionSpec as P

PANELS = 2
PAIR = ("x_lo", "z")
CORE = "core"
ROW = ("x_lo", "z", "core")
COL = ("x_hi", "y")
HI = lax.Precision.HIGHEST

def mm(a, b):
    return lax.dot_general(a, b, (((1,), (0,)), ((), ())), precision=HI, preferred_element_type=jnp.float32)
def mm_nt(a, b):
    return lax.dot_general(a, b, (((1,), (1,)), ((), ())), precision=HI, preferred_element_type=jnp.float32)

STEP = 8

def entries(block):
    columns = [jnp.broadcast_to(block[:, j:j + 1], (STEP, 128)) for j in range(STEP)]
    return [[jnp.broadcast_to(columns[j][i:i + 1, :], (STEP, 128)) for j in range(STEP)] for i in range(STEP)]

def as_columns(x, sub):
    out = []
    for j in range(STEP):
        col = jnp.zeros((STEP, 128), jnp.float32)
        for i in range(STEP):
            if x[i][j] is not None:
                col = jnp.where(sub == i, x[i][j], col)
        out.append(col)
    return out

def apply(cols, rows):
    n = rows.shape[1]
    parts = []
    for c in range(0, n, 128):
        acc = None
        for j in range(STEP):
            t = cols[j] * rows[j:j + 1, c:c + 128]
            acc = t if acc is None else acc + t
        parts.append(acc)
    return jnp.concatenate(parts, 1)

def chol_inverse_8(e):
    x = [[None] * STEP for _ in range(STEP)]
    l = [[None] * STEP for _ in range(STEP)]
    a = [[e[i][j] for j in range(STEP)] for i in range(STEP)]
    inv = [None] * STEP
    for k in range(STEP):
        inv[k] = 1.0 / jnp.sqrt(a[k][k])
        for i in range(k + 1, STEP):
            l[i][k] = a[i][k] * inv[k]
        for j in range(k + 1, STEP):
            for i in range(j, STEP):
                a[i][j] = a[i][j] - l[i][k] * l[j][k]
        x[k][k] = inv[k]
        for j in range(k):
            s = None
            for q in range(j, k):
                t = l[k][q] * x[q][j]
                s = t if s is None else s + t
            x[k][j] = -s * inv[k]
    return x

def inverse_8(e):
    a = [[e[i][j] for j in range(STEP)] for i in range(STEP)]
    for k in range(STEP):
        p = 1.0 / a[k][k]
        a[k] = [a[k][j] * p if j != k else p for j in range(STEP)]
        for i in range(STEP):
            if i == k:
                continue
            f = a[i][k]
            a[i] = [a[i][j] - f * a[k][j] if j != k else -f * p for j in range(STEP)]
    return a

def eliminate(m_ref, n, symmetric):
    lanes8 = lax.broadcasted_iota(jnp.int32, (STEP, n), 1)
    subs8 = lax.broadcasted_iota(jnp.int32, (STEP, n), 0)
    sub = lax.broadcasted_iota(jnp.int32, (STEP, 128), 0)
    lanes = lax.broadcasted_iota(jnp.int32, (n, n), 1)
    rows_of = lax.broadcasted_iota(jnp.int32, (n, n), 0)

    def body(k, _):
        at = pl.multiple_of(k * STEP, STEP)
        rows = m_ref[pl.ds(at, STEP), :]
        block = pltpu.roll(rows, n - at, 1)[:, :STEP]
        here = (lanes8 >= at) & (lanes8 < at + STEP)
        e = entries(block)
        unit = jnp.where(here, (lanes8 - at == subs8).astype(jnp.float32), rows)
        if symmetric:
            x = chol_inverse_8(e)
            kept = apply(as_columns(x, sub), unit)
            xt = [[x[j][i] for j in range(STEP)] for i in range(STEP)]
            spread = apply(as_columns(xt, sub), kept)
        else:
            spread = kept = apply(as_columns(inverse_8(e), sub), unit)
        m = m_ref[...]
        inside = (lanes >= at) & (lanes < at + STEP)
        other = (rows_of >= at + STEP) if symmetric else ((rows_of < at) | (rows_of >= at + STEP))
        left = jnp.where(inside & other, m, 0.0)
        full = jnp.concatenate([spread] * (n // STEP), 0)
        full = jnp.where((rows_of >= at) & (rows_of < at + STEP), full, 0.0)
        m_ref[...] = jnp.where(inside & other, 0.0, m) - mm(left, full)
        m_ref[pl.ds(at, STEP), :] = kept
        return 0

    lax.fori_loop(0, n // STEP, body, 0)

def factor_kernel(gram_ref, top_ref, inv_ref, sign_ref, tf_ref, m_ref):
    n = gram_ref.shape[0]
    r = lax.broadcasted_iota(jnp.int32, (n, n), 0)
    c = lax.broadcasted_iota(jnp.int32, (n, n), 1)
    m_ref[...] = gram_ref[...]
    eliminate(m_ref, n, True)
    inv = jnp.where(r >= c, m_ref[...], 0.0)
    inv_ref[...] = inv
    q1t = mm_nt(inv, top_ref[...])
    diag = jnp.sum(jnp.where(r == c, q1t, 0.0), axis=0, keepdims=True)
    sign = jnp.where(diag >= 0, -1.0, 1.0)
    sign_ref[...] = sign
    m_ref[...] = (r == c).astype(jnp.float32) - q1t * sign
    eliminate(m_ref, n, False)
    tf_ref[...] = m_ref[...]

def factors(gram, top):
    n = gram.shape[0]
    f32 = jnp.float32
    return pl.pallas_call(
        factor_kernel,
        out_shape=[jax.ShapeDtypeStruct((n, n), f32), jax.ShapeDtypeStruct((1, n), f32), jax.ShapeDtypeStruct((n, n), f32)],
        scratch_shapes=[pltpu.VMEM((n, n), f32)],
        compiler_params=pltpu.CompilerParams(vmem_limit_bytes=32 * 2**20),
        cost_estimate=pl.CostEstimate(flops=2 * 64 * n**3, bytes_accessed=20 * n * n, transcendentals=0),
    )(gram, top)


def mm_tn(a, b):
    return lax.dot_general(a, b, (((0,), (0,)), ((), ())), precision=HI, preferred_element_type=jnp.float32)


def swap(x, axis):
    return lax.all_to_all(x, axis, 0, 0, tiled=True)


def gathered(x, axis):
    return swap(jnp.broadcast_to(x[None], (lax.axis_size(axis), *x.shape)), axis)


def other_core(x):
    return lax.ppermute(x, CORE, [(0, 1), (1, 0)])


def in_core_order(mine, core, axis):
    theirs = other_core(mine)
    first = core == 0
    return jnp.stack([jnp.where(first, mine, theirs), jnp.where(first, theirs, mine)], axis)


def to_mirror(piece):
    rows, cols = lax.axis_size(ROW), lax.axis_size(COL)
    pairs = []
    for r in range(rows):
        for c in range(cols):
            to_row, to_col = r // cols * cols + c, r % cols
            pairs.append((r * cols + c, to_row * cols + to_col))
    return lax.ppermute(piece, ROW + COL, pairs)


def cut_rows(x, blocks, peers):
    width = x.shape[-1]
    return x.reshape(blocks, peers, -1, width).transpose(1, 0, 2, 3).reshape(peers, -1, width)


def joined_rows(slabs, blocks):
    peers, _, width = slabs.shape
    return slabs.reshape(peers, blocks, -1, width).transpose(1, 0, 2, 3).reshape(-1, width)


def mirror_rows(mine, core, blocks):
    far, near = lax.axis_size("x_lo"), lax.axis_size("z")
    width = mine.shape[-1]
    both = in_core_order(mine.reshape(far, near, blocks, -1, width), core, 2)
    return both.transpose(3, 0, 1, 2, 4, 5).reshape(-1, width)


def on_device(matrix_tiles):
    tile_shape = matrix_tiles.shape
    blocks, tile, wide = tile_shape[0], tile_shape[2], tile_shape[3]
    band = 2 * tile
    rows, cols = lax.axis_size(ROW), lax.axis_size(COL)
    r, c, core = lax.axis_index(ROW), lax.axis_index(COL), lax.axis_index(CORE)
    a = matrix_tiles.reshape(blocks * tile, wide * tile)
    slab = blocks * tile // cols
    part = band // cols

    def places(count, peers, me):
        at = jnp.arange(count, dtype=jnp.int32)
        return (at // tile * peers + me) * tile + at % tile

    row_of, col_of = places(blocks * tile, rows, r), places(wide * tile, cols, c)
    lane = jnp.arange(band, dtype=jnp.int32)
    for panel in range(PANELS):
        start, below = panel * band, (panel + 1) * band
        source = cut_rows(a[:, :tile], blocks, cols)
        source = swap(source, COL)
        first = start // tile
        piece = jnp.concatenate([source[first], source[first + 1]], 1)
        mirrored = to_mirror(piece)
        p_rows = joined_rows(gathered(piece, COL), blocks)
        p_cols = mirror_rows(gathered(mirrored, PAIR), core, blocks)
        p_rows = jnp.where((row_of >= below)[:, None], p_rows, 0.0)
        p_cols = jnp.where((col_of >= below)[:, None], p_cols, 0.0)

        gram = mm_tn(p_cols, p_cols).reshape(cols, part, band)
        top = jnp.concatenate(
            [jnp.where(c == below // tile + i, p_cols[:tile], 0.0) for i in range(2)], 0
        ).reshape(cols, part, band)
        summed = swap(jnp.concatenate([gram, top], 1), COL).sum(0)
        summed = gathered(summed, COL)
        gram, top = summed[:, :part].reshape(band, band), summed[:, part:].reshape(band, band)
        inverse, sign, tf = factors(gram, top)

        y_rows = mm_nt(p_rows, inverse) - jnp.where(row_of[:, None] - below == lane[None, :], sign, 0.0)
        y_cols = mm_nt(p_cols, inverse) - jnp.where(col_of[:, None] - below == lane[None, :], sign, 0.0)
        u = mm(a, y_cols)
        h = mm_tn(y_rows, u).reshape(cols, part, band)
        sent = jnp.concatenate([cut_rows(u, blocks, cols), h], 1)
        summed = swap(sent, COL).sum(0)
        piece, h = summed[:slab], summed[slab:]
        arrived = gathered(jnp.concatenate([to_mirror(piece), h], 0), PAIR)
        h = arrived[:, slab:].sum(0)
        h = h + other_core(h)
        u_cols = mirror_rows(arrived[:, :slab], core, blocks)
        arrived = gathered(jnp.concatenate([piece, h], 0), COL)
        u_rows = joined_rows(arrived[:, :slab], blocks)
        h = arrived[:, slab:].reshape(band, band)
        half_z = 0.5 * mm_tn(tf, mm(h, tf))
        w_rows = mm(u_rows, tf) - mm(y_rows, half_z)
        w_cols = mm(u_cols, tf) - mm(y_cols, half_z)
        a = a - mm_nt(jnp.concatenate([y_rows, w_rows], 1), jnp.concatenate([w_cols, y_cols], 1))
    return a.reshape(tile_shape)


def solution(mesh):
    finer = Mesh(mesh.devices.reshape(2, 4, 2, 2, 4), ("x_lo", "z", "core", "x_hi", "y"))
    spec = P(None, ROW, None, None, COL, None)
    return jax.shard_map(on_device, mesh=finer, in_specs=(spec,), out_specs=spec, check_vma=False)
```

time: 945 us -> 519 us (0.55)
  other arithmetic: 286 us -> 23.5 us
  waiting for transfers between devices: 235 us -> 65.9 us
  local copies, waits for them, and re-layouts: 168 us -> 44.4 us
  blocking collectives: 50.2 us -> 159 us
  Pallas kernels: 0 us -> 101 us
  matrix products: 102 us -> 42.2 us
  between operations: 19.4 us -> 1.07 us
    another operation x38 -> x4, other arithmetic: 248 us -> 3.24 us  [in_core_order(): jnp.stack([jnp.where(first, mine, theirs), jnp.where(first, theirs, mine)...]
    all_gather x4 -> x0, waiting for transfers between devices: 176 us -> none  [broadcast(): lax.all_gather(shard, axis)]
    all_to_all x4 -> x10, blocking collectives: 50.2 us -> 159 us  [swap(): return lax.all_to_all(x, axis, 0, 0, tiled=True)]
    pallas_call x0 -> x2, Pallas kernels: none -> 101 us  [factors(): pl.pallas_call(factor_kernel, out_shape=[jax.ShapeDtypeStruct((n, n), f32...]
    ppermute x0 -> x10, starting transfers between devices: none -> 39.2 us  [the longest x6 19.9 us: other_core(): return lax.ppermute(x, CORE, [(0, 1), (1, 0)])]
    dot_general x30 -> x24, matrix products: 78.8 us -> 42.2 us  [the longest x6 18.4 us: mm_nt(): lax.dot_general(a, b, (((1,), (1,)), ((), ())), precision=HI, preferred_e...]
    another operation x38 -> x0, local copies, waits for them, and re-layouts: 35.4 us -> none  [the longest x29 29.4 us: lower_inverse(): lax.linalg.triangular_solve(factor, identity, left_side=True, lower=True)]
    all_to_all x14 -> x6, starting transfers between devices: 69.4 us -> 37.6 us  [swap(): return lax.all_to_all(x, axis, 0, 0, tiled=True)]
  transfers between devices with their start and end apart: 18 -> 16, of which waited for: 12 -> 14; matrix products, arithmetic and copies ran while one was open for 26% -> 3% of each run, Pallas kernels for 0% -> 0%
where the time goes in v1:
time: 519 us; the launch traced here: 513 us
  blocking collectives  159 us (31%)
  Pallas kernels  101 us (19%)
  starting transfers between devices  76.8 us (15%)
  waiting for transfers between devices  65.9 us (13%)
  local copies, waits for them, and re-layouts  44.4 us (9%)
  matrix products  42.2 us (8%)
  other arithmetic  23.5 us (5%)
    all_to_all x10, blocking collectives, swap(): return lax.all_to_all(x, axis, 0, 0, tiled=True)  159 us
    pallas_call x2, Pallas kernels, factors(): pl.pallas_call(factor_kernel, out_shape=[jax.ShapeDtypeStruct((n, n), f32...  101 us
    all_to_all x6, waiting for transfers between devices, swap(): return lax.all_to_all(x, axis, 0, 0, tiled=True)  50.6 us
    all_to_all x6, starting transfers between devices, swap(): return lax.all_to_all(x, axis, 0, 0, tiled=True)  37.6 us
    ppermute x6, starting transfers between devices, other_core(): return lax.ppermute(x, CORE, [(0, 1), (1, 0)])  19.9 us
    ppermute x4, starting transfers between devices, to_mirror(): return lax.ppermute(piece, ROW + COL, pairs)  19.4 us
    dot_general x6, matrix products, mm_nt(): lax.dot_general(a, b, (((1,), (1,)), ((), ())), precision=HI, preferred_e...  18.4 us
    dot_general x12, matrix products, mm(): lax.dot_general(a, b, (((1,), (0,)), ((), ())), precision=HI, preferred_e...  16.7 us
  transfers between devices with their start and end apart: 16, of which 14 were waited for; matrix products, arithmetic and copies ran while one was open for 3% of the time, Pallas kernels for 0%

profile of v1, /device:TPU:1, one launch (start us, length us, event | category | flops | bytes accessed | tf_op | source)
XLA Modules:
  0.0 513.5 jit_solution(871205563550578143)
XLA Ops:
  0.0 12.2 %reduce = f32[5,128,10,128]{3,2,1,0:T(8,128)} reduce(f32[5,1,128,10,1,128]{5,4,3,2,1,0:T(1,128)} %param.1, f32[]{:T(128)} %constant.153), dimensions={1,4}, to_apply=%param.1.reduce_sub_computation | reduce | bytes 6553604 | tf_op args[0]
  18.0 15.5 %all_to_all.80 = f32[8,80,128]{2,1,0:T(8,128)S(1)} all-to-all(f32[8,80,128]{2,1,0:T(8,128)S(1)} %bitcast.184), channel_id=1, replica_groups=mesh['x_lo'=2,'z'=4,'core'=2,'x_hi'=2,'y'=4] {'x_hi','y'}, dimensions={0} | all-to-all | bytes 655360 | tf_op jit(solution)/shard_map/all_to_all | solution.py:147
  33.5 4.4 collective-permute-start
  40.1 18.6 %all_to_all.81 = f32[8,80,256]{2,1,0:T(8,128)S(1)} all-to-all(f32[8,80,256]{2,1,0:T(8,128)S(1)} %broadcast_in_dim.161), channel_id=1, replica_groups=mesh['x_lo'=2,'z'=4,'core'=2,'x_hi'=2,'y'=4] {'x_lo','z'}, dimensions={0} | all-to-all | bytes 1310720 | tf_op jit(solution)/shard_map/all_to_all | solution.py:147
  58.7 4.3 collective-permute-start.1
  69.9 12.8 %all_to_all.82 = f32[8,64,256]{2,1,0:T(8,128)S(1)} all-to-all(f32[8,64,256]{2,1,0:T(8,128)S(1)} %pad_maximum_fusion.2), channel_id=1, replica_groups=mesh['x_lo'=2,'z'=4,'core'=2,'x_hi'=2,'y'=4] {'x_hi','y'}, dimensions={0} | all-to-all | bytes 1048576 | tf_op jit(solution)/shard_map/all_to_all | solution.py:147
  87.8 9.5 %all-to-all-done.1 = f32[8,80,256]{2,1,0:T(8,128)S(1)} async-done(((f32[8,80,256]{2,1,0:T(8,128)}), f32[8,80,256]{2,1,0:T(8,128)S(1)}, u32[]{:S(2)}, u32[]{:S(2)}) %all-to-all-start.1) | async-done | bytes 655392 | tf_op jit(solution)/shard_map/all_to_all | solution.py:147
  98.1 6.3 %all-to-all-start.4 = ((f32[8,64,256]{2,1,0:T(8,128)}), f32[8,64,256]{2,1,0:T(8,128)S(1)}, u32[]{:S(2)}, u32[]{:S(2)}) async-start(f32[8,64,256]{2,1,0:T(8,128)} %broadcast_in_dim.166), calls=%async_computation.4 | async-start | bytes 1048576 | tf_op jit(solution)/shard_map/all_to_all | solution.py:147
  106.2 7.3 %all-to-all-done.4 = f32[8,64,256]{2,1,0:T(8,128)S(1)} async-done(((f32[8,64,256]{2,1,0:T(8,128)}), f32[8,64,256]{2,1,0:T(8,128)S(1)}, u32[]{:S(2)}, u32[]{:S(2)}) %all-to-all-start.4) | async-done | bytes 524320 | tf_op jit(solution)/shard_map/all_to_all | solution.py:147
  113.6 50.5 %shard_map.17 = (f32[256,256]{1,0:T(8,128)S(1)}, f32[1,256]{1,0:T(1,128)S(1)}, f32[256,256]{1,0:T(8,128)S(1)}) custom-call(f32[256,256]{1,0:T(8,128)S(1)} %bitcast.149, f32[256,256]{1,0:T(8,128)S(1)} %bitcast.148), custom_call_target="tpu_custom_call" | custom-call | flops 2147483648 | bytes 1310720 | tf_op jit(solution)/shard_map/pallas_call | solution.py:133
  172.0 19.9 %all_to_all.83 = f32[8,112,256]{2,1,0:T(8,128)S(1)} all-to-all(f32[8,112,256]{2,1,0:T(8,128)S(1)} %pad_maximum_fusion), channel_id=1, replica_groups=mesh['x_lo'=2,'z'=4,'core'=2,'x_hi'=2,'y'=4] {'x_hi','y'}, dimensions={0} | all-to-all | bytes 1835008 | tf_op jit(solution)/shard_map/all_to_all | solution.py:147
  198.3 18.7 %all_to_all.84 = f32[8,112,256]{2,1,0:T(8,128)S(1)} all-to-all(f32[8,112,256]{2,1,0:T(8,128)S(1)} %broadcast_in_dim.170), channel_id=1, replica_groups=mesh['x_lo'=2,'z'=4,'core'=2,'x_hi'=2,'y'=4] {'x_lo','z'}, dimensions={0} | all-to-all | bytes 1835008 | tf_op jit(solution)/shard_map/all_to_all | solution.py:147
  217.0 4.5 collective-permute-start.4
  224.3 13.0 %all-to-all-start.7 = ((f32[8,112,256]{2,1,0:T(8,128)}), f32[8,112,256]{2,1,0:T(8,128)}, u32[]{:S(2)}, u32[]{:S(2)}) async-start(f32[8,112,256]{2,1,0:T(8,128)} %broadcast_in_dim.171), calls=%async_computation.7 | async-start | bytes 1835008 | tf_op jit(solution)/shard_map/all_to_all | solution.py:147
  239.1 11.4 %all-to-all-done.7 = f32[8,112,256]{2,1,0:T(8,128)} async-done(((f32[8,112,256]{2,1,0:T(8,128)}), f32[8,112,256]{2,1,0:T(8,128)}, u32[]{:S(2)}, u32[]{:S(2)}) %all-to-all-start.7) | async-done | bytes 917536 | tf_op jit(solution)/shard_map/all_to_all | solution.py:147
  257.5 6.8 %convolution_subtract_fusion.1 = f32[640,1280]{1,0:T(8,128)S(1)} fusion(f32[640,1280]{1,0:T(8,128)S(1)} %bitcast.158, f32[1280,256]{0,1:T(8,128)} %copy-done.5, f32[1280,256]{0,1:T(8,128)S(1)} %convolution_subtract_fusion.4, f32[640,256]{0,1:T(8,128)S(1)} %convolution_subtract_fusion.8, f32[640,256]{0,1:T(8,128)S(1)} %copy-done.11), kind=kOutput, calls=%fused_computation.1 | convolution fusion | flops 5034967040 | bytes 10485760 | tf_op jit(solution)/shard_map/dot_general | solution.py:19
  264.3 13.5 %all_to_all.85 = f32[8,80,128]{2,1,0:T(8,128)S(1)} all-to-all(f32[8,80,128]{2,1,0:T(8,128)S(1)} %bitcast.185), channel_id=1, replica_groups=mesh['x_lo'=2,'z'=4,'core'=2,'x_hi'=2,'y'=4] {'x_hi','y'}, dimensions={0} | all-to-all | bytes 655360 | tf_op jit(solution)/shard_map/all_to_all | solution.py:147
  284.3 16.5 %all_to_all.86 = f32[8,80,256]{2,1,0:T(8,128)} all-to-all(f32[8,80,256]{2,1,0:T(8,128)S(1)} %broadcast_in_dim.175), channel_id=1, replica_groups=mesh['x_lo'=2,'z'=4,'core'=2,'x_hi'=2,'y'=4] {'x_lo','z'}, dimensions={0} | all-to-all | bytes 1310720 | tf_op jit(solution)/shard_map/all_to_all | solution.py:147
  320.4 14.2 %all_to_all.87 = f32[8,64,256]{2,1,0:T(8,128)} all-to-all(f32[8,64,256]{2,1,0:T(8,128)S(1)} %pad_maximum_fusion.3), channel_id=1, replica_groups=mesh['x_lo'=2,'z'=4,'core'=2,'x_hi'=2,'y'=4] {'x_hi','y'}, dimensions={0} | all-to-all | bytes 1048576 | tf_op jit(solution)/shard_map/all_to_all | solution.py:147
  335.6 4.2 all-to-all-start.9
  340.9 8.3 %all-to-all-done.9 = f32[8,80,256]{2,1,0:T(8,128)} async-done(((f32[8,80,256]{2,1,0:T(8,128)}), f32[8,80,256]{2,1,0:T(8,128)}, u32[]{:S(2)}, u32[]{:S(2)}) %all-to-all-start.9) | async-done | bytes 655392 | tf_op jit(solution)/shard_map/all_to_all | solution.py:147
  350.0 5.7 %all-to-all-start.12 = ((f32[8,64,256]{2,1,0:T(8,128)}), f32[8,64,256]{2,1,0:T(8,128)}, u32[]{:S(2)}, u32[]{:S(2)}) async-start(f32[8,64,256]{2,1,0:T(8,128)} %broadcast_in_dim.177), calls=%async_computation.12 | async-start | bytes 1048576 | tf_op jit(solution)/shard_map/all_to_all | solution.py:147
  359.9 4.8 all-to-all-done.12
  365.8 50.5 %shard_map.18 = (f32[256,256]{1,0:T(8,128)S(1)}, f32[1,256]{1,0:T(1,128)S(1)}, f32[256,256]{1,0:T(8,128)S(1)}) custom-call(f32[256,256]{1,0:T(8,128)S(1)} %bitcast.151, f32[256,256]{1,0:T(8,128)S(1)} %bitcast.150), custom_call_target="tpu_custom_call" | custom-call | flops 2147483648 | bytes 1310720 | tf_op jit(solution)/shard_map/pallas_call | solution.py:133
  424.1 15.3 %all_to_all.88 = f32[8,112,256]{2,1,0:T(8,128)} all-to-all(f32[8,112,256]{2,1,0:T(8,128)S(1)} %pad_maximum_fusion.1), channel_id=1, replica_groups=mesh['x_lo'=2,'z'=4,'core'=2,'x_hi'=2,'y'=4] {'x_hi','y'}, dimensions={0} | all-to-all | bytes 1835008 | tf_op jit(solution)/shard_map/all_to_all | solution.py:147
  442.2 6.7 %collective-permute-start.7 = (f32[80,256]{1,0:T(8,128)S(1)}, f32[80,256]{1,0:T(8,128)S(1)}, u32[]{:S(2)}, u32[]{:S(2)}) collective-permute-start(f32[80,256]{1,0:T(8,128)S(1)} %slice.116), channel_id=1, source_target_pairs={{0,0},{1,8},{2,16},{3,24},{4,32},{5,40},{6,48},{7,56},{8,1},{9,9},... | collective-permute-start | bytes 245768 | tf_op jit(solution)/shard_map/ppermute | solution.py:171
  451.9 13.6 %all_to_all.89 = f32[8,112,256]{2,1,0:T(8,128)S(1)} all-to-all(f32[8,112,256]{2,1,0:T(8,128)S(1)} %broadcast_in_dim.181), channel_id=1, replica_groups=mesh['x_lo'=2,'z'=4,'core'=2,'x_hi'=2,'y'=4] {'x_lo','z'}, dimensions={0} | all-to-all | bytes 1835008 | tf_op jit(solution)/shard_map/all_to_all | solution.py:147
  466.4 6.7 %collective-permute-start.9 = (f32[2,4,5,16,256]{4,3,2,1,0:T(8,128)}, f32[2,4,5,16,256]{4,3,2,1,0:T(8,128)}, u32[]{:S(2)}, u32[]{:S(2)}) collective-permute-start(f32[2,4,5,16,256]{4,3,2,1,0:T(8,128)} %bitcast.64), channel_id=1, source_target_pairs={{0,8},{8,0},{1,9},{9,1},{2,10},{10,2},{3,11},{11,3},{4,12},{12,4},... | collective-permute-start | bytes 1966088 | tf_op jit(solution)/shard_map/ppermute | solution.py:155
  475.9 4.2 all-to-all-start.15
  484.3 9.3 %all-to-all-done.15 = f32[8,112,256]{2,1,0:T(8,128)} async-done(((f32[8,112,256]{2,1,0:T(8,128)}), f32[8,112,256]{2,1,0:T(8,128)}, u32[]{:S(2)}, u32[]{:S(2)}) %all-to-all-start.15) | async-done | bytes 917536 | tf_op jit(solution)/shard_map/all_to_all | solution.py:147
  500.1 7.1 %convolution_subtract_fusion = f32[640,1280]{1,0:T(8,128)} fusion(f32[640,1280]{1,0:T(8,128)S(1)} %convolution_subtract_fusion.1, f32[1280,256]{0,1:T(8,128)S(1)} %copy-done.4, f32[1280,256]{0,1:T(8,128)S(1)} %convolution_subtract_fusion.2, f32[640,256]{0,1:T(8,128)S(1)} %convolution_subtract_fusion.6, f32[640,256]{0,1:T(8,128)S(1)} %copy-done.9), kind=kOutput, calls=%fused_computation | convolution fusion | flops 5034967040 | bytes 10485760 | tf_op jit(solution)/shard_map/dot_general | solution.py:19
  507.3 6.0 %reshape.252 = f32[5,1,128,10,1,128]{5,4,3,2,1,0:T(1,128)} reshape(f32[640,1280]{1,0:T(8,128)} %convolution_subtract_fusion) | data formatting | bytes 6553600 | tf_op jit(solution)/shard_map/reshape | solution.py:246
  (164 shorter events, 109.9 us)
Async XLA Ops:
  16.2 1.7 copy-start
  33.5 6.5 %collective-permute-start = (f32[80,256]{1,0:T(8,128)S(1)}, f32[80,256]{1,0:T(8,128)S(1)}, u32[]{:S(2)}, u32[]{:S(2)}) collective-permute-start(f32[80,256]{1,0:T(8,128)S(1)} %pad_maximum_fusion.10), channel_id=1, source_target_pairs={{0,0},{1,8},{2,16},{3,24},{4,32},{5,40},{6,48},{7,56},{8,1},{9,9},... | collective-permute-start | bytes 245768 | tf_op jit(solution)/shard_map/ppermute | solution.py:171
  58.7 6.1 %collective-permute-start.1 = (f32[2,4,5,16,256]{4,3,2,1,0:T(8,128)S(1)}, f32[2,4,5,16,256]{4,3,2,1,0:T(8,128)S(1)}, u32[]{:S(2)}, u32[]{:S(2)}) collective-permute-start(f32[2,4,5,16,256]{4,3,2,1,0:T(8,128)S(1)} %bitcast.180), channel_id=1, source_target_pairs={{0,8},{8,0},{1,9},{9,1},{2,10},{10,2},{3,11},{11,3},{4,12},{12,4},... | collective-permute-start | bytes 1966088 | tf_op jit(solution)/shard_map/ppermute | solution.py:155
  83.6 13.7 %all-to-all-start.1 = ((f32[8,80,256]{2,1,0:T(8,128)}), f32[8,80,256]{2,1,0:T(8,128)S(1)}, u32[]{:S(2)}, u32[]{:S(2)}) async-start(f32[8,80,256]{2,1,0:T(8,128)} %broadcast_in_dim.158), calls=%async_computation.1 | async-start | bytes 1310720 | tf_op jit(solution)/shard_map/all_to_all | solution.py:147
  98.1 15.4 %all-to-all-start.4 = ((f32[8,64,256]{2,1,0:T(8,128)}), f32[8,64,256]{2,1,0:T(8,128)S(1)}, u32[]{:S(2)}, u32[]{:S(2)}) async-start(f32[8,64,256]{2,1,0:T(8,128)} %broadcast_in_dim.166), calls=%async_computation.4 | async-start | bytes 1048576 | tf_op jit(solution)/shard_map/all_to_all | solution.py:147
  113.6 51.9 %copy-start.1 = (f32[80,8,10,128]{3,1,2,0:T(8,128)S(1)}, f32[80,8,10,128]{3,1,2,0:T(8,128)}, u32[]{:S(2)}) copy-start(f32[80,8,10,128]{3,1,2,0:T(8,128)} %copy-done) | copy-start | bytes 9830404
  165.4 90.0 %copy-start.5 = (f32[1280,256]{0,1:T(8,128)}, f32[1280,256]{0,1:T(8,128)S(1)}, u32[]{:S(2)}) copy-start(f32[1280,256]{0,1:T(8,128)S(1)} %convolution_subtract_fusion.5) | copy-start | bytes 3932164
  169.1 1.1 copy-start.14
  171.1 83.4 %copy-start.10 = (f32[640,256]{0,1:T(8,128)}, f32[640,256]{0,1:T(8,128)S(1)}, u32[]{:S(2)}) copy-start(f32[640,256]{0,1:T(8,128)S(1)} %convolution_subtract_fusion.9) | copy-start | bytes 1966084
  192.0 6.2 %collective-permute-start.2 = (f32[80,256]{1,0:T(8,128)S(1)}, f32[80,256]{1,0:T(8,128)S(1)}, u32[]{:S(2)}, u32[]{:S(2)}) collective-permute-start(f32[80,256]{1,0:T(8,128)S(1)} %slice.104), channel_id=1, source_target_pairs={{0,0},{1,8},{2,16},{3,24},{4,32},{5,40},{6,48},{7,56},{8,1},{9,9},... | collective-permute-start | bytes 245768 | tf_op jit(solution)/shard_map/ppermute | solution.py:171
  217.0 20.3 %collective-permute-start.4 = (f32[2,4,5,16,256]{4,3,2,1,0:T(8,128)S(1)}, f32[2,4,5,16,256]{4,3,2,1,0:T(8,128)S(1)}, u32[]{:S(2)}, u32[]{:S(2)}) collective-permute-start(f32[2,4,5,16,256]{4,3,2,1,0:T(8,128)S(1)} %bitcast.182), channel_id=1, source_target_pairs={{0,8},{8,0},{1,9},{9,1},{2,10},{10,2},{3,11},{11,3},{4,12},{12,4},... | collective-permute-start | bytes 1966088 | tf_op jit(solution)/shard_map/ppermute | solution.py:155
  221.5 1.8 collective-permute-start.3
  224.3 26.2 %all-to-all-start.7 = ((f32[8,112,256]{2,1,0:T(8,128)}), f32[8,112,256]{2,1,0:T(8,128)}, u32[]{:S(2)}, u32[]{:S(2)}) async-start(f32[8,112,256]{2,1,0:T(8,128)} %broadcast_in_dim.171), calls=%async_computation.7 | async-start | bytes 1835008 | tf_op jit(solution)/shard_map/all_to_all | solution.py:147
  255.4 1.9 copy-start.2
  255.4 2.1 copy-start.11
  277.9 4.2 copy-start.16
  277.9 6.3 %collective-permute-start.5 = (f32[80,256]{1,0:T(8,128)S(1)}, f32[80,256]{1,0:T(8,128)S(1)}, u32[]{:S(2)}, u32[]{:S(2)}) collective-permute-start(f32[80,256]{1,0:T(8,128)S(1)} %pad_maximum_fusion.11), channel_id=1, source_target_pairs={{0,0},{1,8},{2,16},{3,24},{4,32},{5,40},{6,48},{7,56},{8,1},{9,9},... | collective-permute-start | bytes 245768 | tf_op jit(solution)/shard_map/ppermute | solution.py:171
  300.8 6.2 %collective-permute-start.6 = (f32[2,4,5,16,256]{4,3,2,1,0:T(8,128)}, f32[2,4,5,16,256]{4,3,2,1,0:T(8,128)}, u32[]{:S(2)}, u32[]{:S(2)}) collective-permute-start(f32[2,4,5,16,256]{4,3,2,1,0:T(8,128)} %bitcast.43), channel_id=1, source_target_pairs={{0,8},{8,0},{1,9},{9,1},{2,10},{10,2},{3,11},{11,3},{4,12},{12,4},... | collective-permute-start | bytes 1966088 | tf_op jit(solution)/shard_map/ppermute | solution.py:155
  317.4 3.0 copy-start.15
  320.4 14.3 %copy-start.17 = (f32[80,256]{1,0:T(8,128)S(1)}, f32[80,256]{1,0:T(8,128)}, u32[]{:S(2)}) copy-start(f32[80,256]{1,0:T(8,128)} %copy-done.16) | copy-start | bytes 245764
  335.6 13.6 %all-to-all-start.9 = ((f32[8,80,256]{2,1,0:T(8,128)}), f32[8,80,256]{2,1,0:T(8,128)}, u32[]{:S(2)}, u32[]{:S(2)}) async-start(f32[8,80,256]{2,1,0:T(8,128)} %broadcast_in_dim.173), calls=%async_computation.9 | async-start | bytes 1310720 | tf_op jit(solution)/shard_map/all_to_all | solution.py:147
  350.0 14.7 %all-to-all-start.12 = ((f32[8,64,256]{2,1,0:T(8,128)}), f32[8,64,256]{2,1,0:T(8,128)}, u32[]{:S(2)}, u32[]{:S(2)}) async-start(f32[8,64,256]{2,1,0:T(8,128)} %broadcast_in_dim.177), calls=%async_computation.12 | async-start | bytes 1048576 | tf_op jit(solution)/shard_map/all_to_all | solution.py:147
  365.7 50.5 %copy-start.7 = (f32[1280,256]{0,1:T(8,128)S(1)}, f32[1280,256]{0,1:T(8,128)}, u32[]{:S(2)}) copy-start(f32[1280,256]{0,1:T(8,128)} %copy-done.6) | copy-start | bytes 3932164
  417.6 2.8 copy-start.3
  420.4 1.1 copy-start.13
  442.2 9.6 %collective-permute-start.7 = (f32[80,256]{1,0:T(8,128)S(1)}, f32[80,256]{1,0:T(8,128)S(1)}, u32[]{:S(2)}, u32[]{:S(2)}) collective-permute-start(f32[80,256]{1,0:T(8,128)S(1)} %slice.116), channel_id=1, source_target_pairs={{0,0},{1,8},{2,16},{3,24},{4,32},{5,40},{6,48},{7,56},{8,1},{9,9},... | collective-permute-start | bytes 245768 | tf_op jit(solution)/shard_map/ppermute | solution.py:171
  466.4 13.7 %collective-permute-start.9 = (f32[2,4,5,16,256]{4,3,2,1,0:T(8,128)}, f32[2,4,5,16,256]{4,3,2,1,0:T(8,128)}, u32[]{:S(2)}, u32[]{:S(2)}) collective-permute-start(f32[2,4,5,16,256]{4,3,2,1,0:T(8,128)} %bitcast.64), channel_id=1, source_target_pairs={{0,8},{8,0},{1,9},{9,1},{2,10},{10,2},{3,11},{11,3},{4,12},{12,4},... | collective-permute-start | bytes 1966088 | tf_op jit(solution)/shard_map/ppermute | solution.py:155
  473.1 1.8 collective-permute-start.8
  475.9 17.7 %all-to-all-start.15 = ((f32[8,112,256]{2,1,0:T(8,128)}), f32[8,112,256]{2,1,0:T(8,128)}, u32[]{:S(2)}, u32[]{:S(2)}) async-start(f32[8,112,256]{2,1,0:T(8,128)} %broadcast_in_dim.182), calls=%async_computation.15 | async-start | bytes 1835008 | tf_op jit(solution)/shard_map/all_to_all | solution.py:147
  495.6 2.1 copy-start.9
  497.1 1.5 copy-start.4
  497.1 1.7 copy-start.12
  (3 other events, 3.0 us)
